TPU v7x, 32 devices: a whole 2x2x4 slice. The times are simulated.
32 devices in a mesh: wide: 4 (over y, core), narrow: 8 (over z, x).
Axes of the slice: x: 2, y: 2, z: 4, core: 2. Of those that a mesh axis runs over, the one named last changes fastest.
Arguments:
- leaf_rhs: bfloat16 [64, 1024, 256], P('wide', 'narrow'), may hold values from -6 to 6
- leaf_inv: bfloat16 [64, 256, 256], P('wide', 'narrow'), may hold values from -0.375 to 0.375
- leaf_upd: bfloat16 [64, 5, 256, 256], P('wide', None, 'narrow'), may hold values from -0.0390625 to 0.0390625
- leaf_targets: int32 [64, 5], P('wide'), may hold values from 0 to 2
- sep_rhs: bfloat16 [3, 1024, 256], P(None, 'narrow'), may hold values from -6 to 6
- sep_inv: bfloat16 [3, 256, 256], replicated, may hold values from -0.375 to 0.375
- sep_low: bfloat16 [3, 256, 256], replicated, may hold values from -0.21875 to 0.21875
Outputs:
- leaf_sol: bfloat16 [64, 1024, 256], P('wide', 'narrow')
- sep_sol: bfloat16 [3, 1024, 256], P(None, 'narrow')
All inputs are finite; a program needn't handle non-finite values.
Results may differ from a plain program's by a relative error of at most 0.012.
Values may be sent and summed in bfloat16 or wider, within the bound.
A program may use at most 64 MiB of HBM per device.

v0:
```python
import jax
import jax.numpy as jnp
from jax import lax
from jax.sharding import PartitionSpec as P


def separator_solve(gathered, sep_rhs, sep_inv, sep_low):
    nsep = sep_inv.shape[0]
    solved_list = []
    for row in range(nsep):
        reduced = sep_rhs[row].astype(jnp.float32) - gathered[row]
        for col in range(row):
            reduced = reduced - jnp.dot(
                solved_list[col],
                sep_low[row * (row - 1) // 2 + col],
                preferred_element_type=jnp.float32,
            )
        reduced = reduced.astype(jnp.bfloat16)
        solved_list.append(
            jnp.dot(reduced, sep_inv[row], preferred_element_type=jnp.float32).astype(jnp.bfloat16)
        )
    return jnp.stack(solved_list)


def body(leaf_rhs, leaf_inv, leaf_upd, leaf_targets, sep_rhs, sep_inv, sep_low):
    nsep = sep_inv.shape[0]
    nupd = leaf_upd.shape[1]
    leaves, scenarios, width = leaf_rhs.shape
    onehot = (leaf_targets[:, :, None] == jnp.arange(nsep, dtype=jnp.int32)[None, None, :]).astype(
        jnp.float32
    )
    columns = leaf_rhs
    leaf_sol = jnp.einsum(
        "lcj,lji->lci",
        columns,
        lax.all_gather(leaf_inv, "narrow", axis=1, tiled=True),
        preferred_element_type=jnp.float32,
    ).astype(jnp.bfloat16)
    start_sum = jnp.zeros((nsep, scenarios, width), jnp.float32)
    total = start_sum
    piece = lax.all_gather(leaf_upd, "narrow", axis=2, tiled=True)
    columns = leaf_sol
    for block in range(nupd):
        contrib = jnp.einsum(
            "lcj,lji->lci", columns, piece[:, block], preferred_element_type=jnp.float32
        )
        total = total + jnp.einsum("lci,ls->sci", contrib, onehot[:, block])
    gathered = total
    total = lax.psum(gathered, "wide")
    sep_sol = separator_solve(total, sep_rhs, sep_inv, sep_low)
    return (leaf_sol, sep_sol)


def solution(mesh):
    in_specs = (
        P("wide", "narrow", None),
        P("wide", "narrow", None),
        P("wide", None, "narrow", None),
        P("wide", None),
        P(None, "narrow", None),
        P(),
        P(),
    )
    out_specs = (P("wide", "narrow", None), P(None, "narrow", None))
    return jax.shard_map(body, mesh=mesh, in_specs=in_specs, out_specs=out_specs, check_vma=False)
```

profile of v0, /device:TPU:0, one launch (start us, length us, event | category | flops | bytes accessed | tf_op | source)
XLA Modules:
  0.0 266.1 jit_solution(2337355595048886722)
XLA Ops:
  7.2 0.0 copy-start
  7.2 0.0 all-gather.3.cloned.1.call-start
  7.2 0.7 all-gather.3.cloned.1.call-update
  7.9 0.0 all-gather.5.cloned.1.call-start
  8.0 0.7 all-gather.5.cloned.1.call-update
  8.7 0.0 all-reduce.2.cloned.1.call-start
  8.7 0.7 iota_compare_fusion
  9.4 52.8 %all-gather.3.cloned.1.call-done = bf16[16,256,256]{2,1,0:T(8,128)(2,1)} async-done(((bf16[16,32,256]{2,1,0:T(8,128)(2,1)}), bf16[16,256,256]{2,1,0:T(8,128)(2,1)}) %all-gather.3.cloned.1.call-update) | async-done | bytes 2097168 | tf_op jit(solution)/shard_map/all_gather | solution.py:36
  62.2 0.0 copy-done
  62.2 2.0 convolution_convert_fusion
  64.2 0.0 copy-start.1
  64.3 149.5 %all-gather.5.cloned.1.call-done = bf16[16,5,256,256]{3,2,1,0:T(8,128)(2,1)} async-done(((bf16[16,5,32,256]{3,2,1,0:T(8,128)(2,1)}), bf16[16,5,256,256]{3,2,1,0:T(8,128)(2,1)}) %all-gather.5.cloned.1.call-update) | async-done | bytes 10485776 | tf_op jit(solution)/shard_map/all_gather | solution.py:41
  213.8 0.0 copy-start.2
  213.8 2.2 fusion.3
  216.0 0.7 fusion.11
  216.6 2.7 %fusion.1 = bf16[16,128,256]{2,1,0:T(8,128)(2,1)S(1)} fusion(bf16[16,128,256]{2,1,0:T(8,128)(2,1)S(1)} %convolution_convert_fusion, bf16[16,5,256,256]{3,2,1,0:T(8,128)(2,1)} %all-gather.5.cloned.1.call-done), kind=kOutput, calls=%fused_computation.3 | convolution fusion | flops 268435456 | bytes 4194304 | tf_op jit(solution)/shard_map/lcj,lji->lci/dot_general | solution.py:44
  219.4 0.7 fusion.7
  220.1 0.0 copy-done.2
  220.1 0.5 fusion.2
  220.5 0.7 fusion.9
  221.2 0.5 fusion.4
  221.7 0.8 fusion.21
  222.4 0.0 copy-done.1
  222.4 0.5 fusion
  222.9 0.0 copy-start.5
  222.9 0.0 copy-start.4
  222.9 0.0 copy-start.3
  222.9 1.5 fusion.24
  224.4 0.0 all-reduce.2.cloned.1.call-update
  224.4 0.0 copy-done.5
  224.5 31.5 %all-reduce.2.cloned.1.call-done = f32[3,128,256]{2,0,1:T(4,128)} async-done(((f32[3,128,256]{2,0,1:T(4,128)}), f32[3,128,256]{2,0,1:T(4,128)}) %all-reduce.2.cloned.1.call-update) | async-done | bytes 393232 | tf_op jit(solution)/shard_map/psum | solution.py:49
  256.0 1.9 slice_subtract_fusion.1
  257.9 0.0 copy-done.4
  257.9 0.2 convolution_convert_fusion.3
  258.1 0.0 copy-done.3
  258.1 0.3 convolution_convert_fusion.2
  258.4 0.2 convolution_subtract_fusion.1
  258.6 0.3 fusion.29
  258.9 0.7 pad_maximum_fusion
  (1 shorter events, 0.0 us)
Async XLA Ops:
  7.2 55.0 %copy-start = (bf16[16,128,256]{2,1,0:T(8,128)(2,1)S(1)}, bf16[16,128,256]{2,1,0:T(8,128)(2,1)}, u32[]{:S(2)}) copy-start(bf16[16,128,256]{2,1,0:T(8,128)(2,1)} %param.7) | copy-start | bytes 3145732
  7.2 55.0 %all-gather.3.cloned.1.call-start = ((), (), s32[]{:S(2)}) async-start(), calls=%async_computation | async-start | bytes 2359296 | tf_op jit(solution)/shard_map/all_gather | solution.py:36
  7.9 205.8 %all-gather.5.cloned.1.call-start = ((), (), s32[]{:S(2)}) async-start(), calls=%async_computation.1 | async-start | bytes 11796480 | tf_op jit(solution)/shard_map/all_gather | solution.py:41
  8.7 247.4 %all-reduce.2.cloned.1.call-start = ((), (), s32[]{:S(2)}) async-start(), calls=%async_computation.2 | async-start | bytes 1048576 | tf_op jit(solution)/shard_map/psum | solution.py:49
  64.2 158.2 %copy-start.1 = (bf16[16,128,256]{2,1,0:T(8,128)(2,1)}, bf16[16,128,256]{2,1,0:T(8,128)(2,1)S(1)}, u32[]{:S(2)}) copy-start(bf16[16,128,256]{2,1,0:T(8,128)(2,1)S(1)} %convolution_convert_fusion) | copy-start | bytes 3145732
  213.8 6.3 %copy-start.2 = (bf16[16,5,256,256]{3,2,1,0:T(8,128)(2,1)S(1)}, bf16[16,5,256,256]{3,2,1,0:T(8,128)(2,1)}, u32[]{:S(2)}) copy-start(bf16[16,5,256,256]{3,2,1,0:T(8,128)(2,1)} %all-gather.5.cloned.1.call-done) | copy-start | bytes 31457284
  222.9 1.6 copy-start.5
  222.9 35.0 %copy-start.4 = (bf16[3,256,256]{2,1,0:T(8,128)(2,1)S(1)}, bf16[3,256,256]{2,1,0:T(8,128)(2,1)}, u32[]{:S(2)}) copy-start(bf16[3,256,256]{2,1,0:T(8,128)(2,1)} %param.12) | copy-start | bytes 1179652
  222.9 35.2 %copy-start.3 = (bf16[3,256,256]{2,1,0:T(8,128)(2,1)S(1)}, bf16[3,256,256]{2,1,0:T(8,128)(2,1)}, u32[]{:S(2)}) copy-start(bf16[3,256,256]{2,1,0:T(8,128)(2,1)} %param.13) | copy-start | bytes 1179652
Sparse Core Ops, SparseCore 0:
  10.2 51.9 all-gather.2
  64.4 149.3 all-gather.4
  224.6 31.4 all-reduce.1
where the time goes:
time: 266 us
  waiting for transfers between devices  235 us (88%)
  between operations  13.9 us (5%)
  matrix products  13.5 us (5%)
  other arithmetic  3.29 us (1%)
    all_gather x1, waiting for transfers between devices, body(): piece = lax.all_gather(leaf_upd, 'narrow', axis=2, tiled=True)  150 us
    all_gather x1, waiting for transfers between devices, body(): lax.all_gather(leaf_inv, 'narrow', axis=1, tiled=True)  52.8 us
    psum x1, waiting for transfers between devices, body(): total = lax.psum(gathered, 'wide')  31.5 us
    dot_general x5, matrix products, body(): jnp.einsum('lcj,lji->lci', columns, piece[:, block], preferred_element_ty...  6.28 us
  transfers between devices with their start and end apart: 3, of which 3 were waited for; matrix products, arithmetic and copies ran while one was open for 1% of the time, Pallas kernels for 0%

commit v1 on v0

--- a/solution.py
+++ b/solution.py
@@ -2,6 +2,18 @@
 import jax.numpy as jnp
 from jax import lax
 from jax.sharding import PartitionSpec as P
+
+
+def summed_around(value, axis, dim, product):
+    size, index = (lax.axis_size(axis), lax.axis_index(axis))
+    behind = [(i, (i - 1) % size) for i in range(size)]
+    width = value.shape[dim]
+    held = value
+    total = product(held, index * width)
+    for lap in range(1, size):
+        held = lax.ppermute(held, axis, behind)
+        total = total + product(held, (index + lap) % size * width)
+    return total
 
 
 def separator_solve(gathered, sep_rhs, sep_inv, sep_low):
@@ -30,11 +42,16 @@
         jnp.float32
     )
     columns = leaf_rhs
-    leaf_sol = jnp.einsum(
-        "lcj,lji->lci",
-        columns,
-        lax.all_gather(leaf_inv, "narrow", axis=1, tiled=True),
-        preferred_element_type=jnp.float32,
+    leaf_sol = summed_around(
+        leaf_inv,
+        "narrow",
+        1,
+        lambda own_block, offset: jnp.einsum(
+            "lcj,lji->lci",
+            lax.dynamic_slice_in_dim(columns, offset, own_block.shape[1], axis=2),
+            own_block,
+            preferred_element_type=jnp.float32,
+        ),
     ).astype(jnp.bfloat16)
     start_sum = jnp.zeros((nsep, scenarios, width), jnp.float32)
     total = start_sum

time: 266 us -> 244 us (0.917)
  waiting for transfers between devices: 235 us -> 173 us
  starting transfers between devices: 0.11 us -> 37.1 us
  matrix products: 13.5 us -> 16.8 us
    all_gather x1, waiting for transfers between devices: 150 us -> 78 us  [body(): piece = lax.all_gather(leaf_upd, 'narrow', axis=2, tiled=True)]
    ppermute x0 -> x7, waiting for transfers between devices: none -> 59 us  [summed_around(): held = lax.ppermute(held, axis, behind)]
    all_gather x1 -> x0, waiting for transfers between devices: 52.8 us -> none  [body(): lax.all_gather(leaf_inv, 'narrow', axis=1, tiled=True)]
    ppermute x0 -> x7, starting transfers between devices: none -> 37 us  [summed_around(): held = lax.ppermute(held, axis, behind)]
    psum x1, waiting for transfers between devices: 31.5 us -> 34.9 us  [body(): total = lax.psum(gathered, 'wide')]
    dot_general x1 -> x8, matrix products: 2.03 us -> 5.31 us  [body(): jnp.einsum('lcj,lji->lci', lax.dynamic_slice_in_dim(columns, offset, own_...]
  transfers between devices with their start and end apart: 3 -> 9, of which waited for: 3 -> 9; matrix products, arithmetic and copies ran while one was open for 1% -> 2% of each run, Pallas kernels for 0% -> 0%
where the time goes in v1:
time: 244 us
  waiting for transfers between devices  173 us (71%)
  starting transfers between devices  37.1 us (15%)
  matrix products  16.8 us (7%)
  between operations  14.3 us (6%)
  other arithmetic  3.37 us (1%)
    all_gather x1, waiting for transfers between devices, body(): piece = lax.all_gather(leaf_upd, 'narrow', axis=2, tiled=True)  78 us
    ppermute x7, waiting for transfers between devices, summed_around(): held = lax.ppermute(held, axis, behind)  59 us
    ppermute x7, starting transfers between devices, summed_around(): held = lax.ppermute(held, axis, behind)  37 us
    psum x1, waiting for transfers between devices, body(): total = lax.psum(gathered, 'wide')  34.9 us
    dot_general x5, matrix products, body(): jnp.einsum('lcj,lji->lci', columns, piece[:, block], preferred_element_ty...  6.28 us
    dot_general x8, matrix products, body(): jnp.einsum('lcj,lji->lci', lax.dynamic_slice_in_dim(columns, offset, own_...  5.31 us
  transfers between devices with their start and end apart: 9, of which 9 were waited for; matrix products, arithmetic and copies ran while one was open for 2% of the time, Pallas kernels for 0%

profile of v1, /device:TPU:0, one launch (start us, length us, event | category | flops | bytes accessed | tf_op | source)
XLA Modules:
  0.0 244.2 jit_solution(5240795898911319271)
XLA Ops:
  7.2 0.0 copy-start
  7.2 0.0 all-gather.2.cloned.1.call-start
  7.2 0.7 all-gather.2.cloned.1.call-update
  7.9 0.0 all-reduce.2.cloned.1.call-start
  8.0 6.0 %collective-permute-start = (bf16[16,32,256]{2,1,0:T(8,128)(2,1)}, bf16[16,32,256]{2,1,0:T(8,128)(2,1)S(1)}, u32[]{:S(2)}, u32[]{:S(2)}) collective-permute-start(bf16[16,32,256]{2,1,0:T(8,128)(2,1)} %param.8), channel_id=1, source_target_pairs={{0,7},{1,0},{2,1},{3,2},{4,3},{5,4},{6,5},{7,6},{8,15},{9,8},{10,9... | collective-permute-start | bytes 786440 | tf_op jit(solution)/shard_map/ppermute | solution.py:14
  14.0 0.7 iota_compare_fusion
  14.7 0.0 copy-done
  14.7 1.4 fusion.43
  16.1 3.7 %collective-permute-done = bf16[16,32,256]{2,1,0:T(8,128)(2,1)S(1)} collective-permute-done((bf16[16,32,256]{2,1,0:T(8,128)(2,1)}, bf16[16,32,256]{2,1,0:T(8,128)(2,1)S(1)}, u32[]{:S(2)}, u32[]{:S(2)}) %collective-permute-start) | collective-permute-done | bytes 262176 | tf_op jit(solution)/shard_map/ppermute | solution.py:14
  19.9 5.1 %collective-permute-start.1 = (bf16[16,32,256]{2,1,0:T(8,128)(2,1)S(1)}, bf16[16,32,256]{2,1,0:T(8,128)(2,1)S(1)}, u32[]{:S(2)}, u32[]{:S(2)}) collective-permute-start(bf16[16,32,256]{2,1,0:T(8,128)(2,1)S(1)} %collective-permute-done), channel_id=1, source_target_pairs={{0,7},{1,0},{2,1},{3,2},{4,3},{5,4},{6,5},{7,6},{8,15},{9,8},{10,9... | collective-permute-start | bytes 786440 | tf_op jit(solution)/shard_map/ppermute | solution.py:14
  24.9 0.5 fusion.41
  25.4 11.1 %collective-permute-done.1 = bf16[16,32,256]{2,1,0:T(8,128)(2,1)S(1)} collective-permute-done((bf16[16,32,256]{2,1,0:T(8,128)(2,1)S(1)}, bf16[16,32,256]{2,1,0:T(8,128)(2,1)S(1)}, u32[]{:S(2)}, u32[]{:S(2)}) %collective-permute-start.1) | collective-permute-done | bytes 262176 | tf_op jit(solution)/shard_map/ppermute | solution.py:14
  36.5 5.2 %collective-permute-start.2 = (bf16[16,32,256]{2,1,0:T(8,128)(2,1)S(1)}, bf16[16,32,256]{2,1,0:T(8,128)(2,1)S(1)}, u32[]{:S(2)}, u32[]{:S(2)}) collective-permute-start(bf16[16,32,256]{2,1,0:T(8,128)(2,1)S(1)} %collective-permute-done.1), channel_id=1, source_target_pairs={{0,7},{1,0},{2,1},{3,2},{4,3},{5,4},{6,5},{7,6},{8,15},{9,8},{10,9... | collective-permute-start | bytes 786440 | tf_op jit(solution)/shard_map/ppermute | solution.py:14
  41.7 0.5 fusion.39
  42.2 10.8 %collective-permute-done.2 = bf16[16,32,256]{2,1,0:T(8,128)(2,1)S(1)} collective-permute-done((bf16[16,32,256]{2,1,0:T(8,128)(2,1)S(1)}, bf16[16,32,256]{2,1,0:T(8,128)(2,1)S(1)}, u32[]{:S(2)}, u32[]{:S(2)}) %collective-permute-start.2) | collective-permute-done | bytes 262176 | tf_op jit(solution)/shard_map/ppermute | solution.py:14
  53.0 5.2 %collective-permute-start.3 = (bf16[16,32,256]{2,1,0:T(8,128)(2,1)S(1)}, bf16[16,32,256]{2,1,0:T(8,128)(2,1)S(1)}, u32[]{:S(2)}, u32[]{:S(2)}) collective-permute-start(bf16[16,32,256]{2,1,0:T(8,128)(2,1)S(1)} %collective-permute-done.2), channel_id=1, source_target_pairs={{0,7},{1,0},{2,1},{3,2},{4,3},{5,4},{6,5},{7,6},{8,15},{9,8},{10,9... | collective-permute-start | bytes 786440 | tf_op jit(solution)/shard_map/ppermute | solution.py:14
  58.2 0.5 fusion.37
  58.7 10.5 %collective-permute-done.3 = bf16[16,32,256]{2,1,0:T(8,128)(2,1)S(1)} collective-permute-done((bf16[16,32,256]{2,1,0:T(8,128)(2,1)S(1)}, bf16[16,32,256]{2,1,0:T(8,128)(2,1)S(1)}, u32[]{:S(2)}, u32[]{:S(2)}) %collective-permute-start.3) | collective-permute-done | bytes 262176 | tf_op jit(solution)/shard_map/ppermute | solution.py:14
  69.2 5.2 %collective-permute-start.4 = (bf16[16,32,256]{2,1,0:T(8,128)(2,1)S(1)}, bf16[16,32,256]{2,1,0:T(8,128)(2,1)S(1)}, u32[]{:S(2)}, u32[]{:S(2)}) collective-permute-start(bf16[16,32,256]{2,1,0:T(8,128)(2,1)S(1)} %collective-permute-done.3), channel_id=1, source_target_pairs={{0,7},{1,0},{2,1},{3,2},{4,3},{5,4},{6,5},{7,6},{8,15},{9,8},{10,9... | collective-permute-start | bytes 786440 | tf_op jit(solution)/shard_map/ppermute | solution.py:14
  74.4 0.5 fusion.35
  74.9 10.2 %collective-permute-done.4 = bf16[16,32,256]{2,1,0:T(8,128)(2,1)S(1)} collective-permute-done((bf16[16,32,256]{2,1,0:T(8,128)(2,1)S(1)}, bf16[16,32,256]{2,1,0:T(8,128)(2,1)S(1)}, u32[]{:S(2)}, u32[]{:S(2)}) %collective-permute-start.4) | collective-permute-done | bytes 262176 | tf_op jit(solution)/shard_map/ppermute | solution.py:14
  85.1 5.2 %collective-permute-start.5 = (bf16[16,32,256]{2,1,0:T(8,128)(2,1)S(1)}, bf16[16,32,256]{2,1,0:T(8,128)(2,1)S(1)}, u32[]{:S(2)}, u32[]{:S(2)}) collective-permute-start(bf16[16,32,256]{2,1,0:T(8,128)(2,1)S(1)} %collective-permute-done.4), channel_id=1, source_target_pairs={{0,7},{1,0},{2,1},{3,2},{4,3},{5,4},{6,5},{7,6},{8,15},{9,8},{10,9... | collective-permute-start | bytes 786440 | tf_op jit(solution)/shard_map/ppermute | solution.py:14
  90.3 0.5 fusion.33
  90.8 3.4 %collective-permute-done.5 = bf16[16,32,256]{2,1,0:T(8,128)(2,1)S(1)} collective-permute-done((bf16[16,32,256]{2,1,0:T(8,128)(2,1)S(1)}, bf16[16,32,256]{2,1,0:T(8,128)(2,1)S(1)}, u32[]{:S(2)}, u32[]{:S(2)}) %collective-permute-start.5) | collective-permute-done | bytes 262176 | tf_op jit(solution)/shard_map/ppermute | solution.py:14
  94.2 5.2 %collective-permute-start.6 = (bf16[16,32,256]{2,1,0:T(8,128)(2,1)S(1)}, bf16[16,32,256]{2,1,0:T(8,128)(2,1)S(1)}, u32[]{:S(2)}, u32[]{:S(2)}) collective-permute-start(bf16[16,32,256]{2,1,0:T(8,128)(2,1)S(1)} %collective-permute-done.5), channel_id=1, source_target_pairs={{0,7},{1,0},{2,1},{3,2},{4,3},{5,4},{6,5},{7,6},{8,15},{9,8},{10,9... | collective-permute-start | bytes 786440 | tf_op jit(solution)/shard_map/ppermute | solution.py:14
  99.3 0.5 fusion.31
  99.8 9.3 %collective-permute-done.6 = bf16[16,32,256]{2,1,0:T(8,128)(2,1)S(1)} collective-permute-done((bf16[16,32,256]{2,1,0:T(8,128)(2,1)S(1)}, bf16[16,32,256]{2,1,0:T(8,128)(2,1)S(1)}, u32[]{:S(2)}, u32[]{:S(2)}) %collective-permute-start.6) | collective-permute-done | bytes 262176 | tf_op jit(solution)/shard_map/ppermute | solution.py:14
  109.1 0.9 add_convert_fusion
  110.0 0.0 copy-start.1
  110.0 78.0 %all-gather.2.cloned.1.call-done = bf16[16,5,256,256]{3,2,1,0:T(8,128)(2,1)} async-done(((bf16[16,5,32,256]{3,2,1,0:T(8,128)(2,1)}), bf16[16,5,256,256]{3,2,1,0:T(8,128)(2,1)}) %all-gather.2.cloned.1.call-update) | async-done | bytes 10485776 | tf_op jit(solution)/shard_map/all_gather | solution.py:58
  188.1 0.0 copy-start.2
  188.1 2.2 fusion.3
  190.3 0.7 fusion.11
  190.9 2.7 %fusion.1 = bf16[16,128,256]{2,1,0:T(8,128)(2,1)S(1)} fusion(bf16[16,128,256]{2,1,0:T(8,128)(2,1)S(1)} %add_convert_fusion, bf16[16,5,256,256]{3,2,1,0:T(8,128)(2,1)} %all-gather.2.cloned.1.call-done), kind=kOutput, calls=%fused_computation.3 | convolution fusion | flops 268435456 | bytes 4194304 | tf_op jit(solution)/shard_map/lcj,lji->lci/dot_general | solution.py:61
  193.7 0.7 fusion.7
  194.4 0.0 copy-done.2
  194.4 0.5 fusion.2
  194.8 0.7 fusion.9
  195.5 0.5 fusion.4
  196.0 0.8 fusion.21
  196.7 0.0 copy-done.1
  196.7 0.5 fusion
  197.2 0.0 copy-start.5
  197.2 0.0 copy-start.4
  197.2 0.0 copy-start.3
  197.2 1.5 fusion.24
  198.7 0.0 all-reduce.2.cloned.1.call-update
  198.7 0.0 copy-done.5
  198.8 34.9 %all-reduce.2.cloned.1.call-done = f32[3,128,256]{2,0,1:T(4,128)} async-done(((f32[3,128,256]{2,0,1:T(4,128)}), f32[3,128,256]{2,0,1:T(4,128)}) %all-reduce.2.cloned.1.call-update) | async-done | bytes 393232 | tf_op jit(solution)/shard_map/psum | solution.py:66
  233.7 2.0 slice_subtract_fusion.1
  235.7 0.0 copy-done.4
  235.7 0.2 convolution_convert_fusion.2
  235.8 0.0 copy-done.3
  235.9 0.3 convolution_convert_fusion.1
  236.2 0.2 convolution_subtract_fusion.1
  236.3 0.3 fusion.29
  236.6 0.7 pad_maximum_fusion
  (1 shorter events, 0.0 us)
Async XLA Ops:
  7.2 7.5 %copy-start = (bf16[16,128,256]{2,1,0:T(8,128)(2,1)S(1)}, bf16[16,128,256]{2,1,0:T(8,128)(2,1)}, u32[]{:S(2)}) copy-start(bf16[16,128,256]{2,1,0:T(8,128)(2,1)} %param.7) | copy-start | bytes 3145732
  7.2 180.9 %all-gather.2.cloned.1.call-start = ((), (), s32[]{:S(2)}) async-start(), calls=%async_computation | async-start | bytes 11796480 | tf_op jit(solution)/shard_map/all_gather | solution.py:58
  7.9 225.8 %all-reduce.2.cloned.1.call-start = ((), (), s32[]{:S(2)}) async-start(), calls=%async_computation.1 | async-start | bytes 1048576 | tf_op jit(solution)/shard_map/psum | solution.py:66
  8.0 11.9 %collective-permute-start = (bf16[16,32,256]{2,1,0:T(8,128)(2,1)}, bf16[16,32,256]{2,1,0:T(8,128)(2,1)S(1)}, u32[]{:S(2)}, u32[]{:S(2)}) collective-permute-start(bf16[16,32,256]{2,1,0:T(8,128)(2,1)} %param.8), channel_id=1, source_target_pairs={{0,7},{1,0},{2,1},{3,2},{4,3},{5,4},{6,5},{7,6},{8,15},{9,8},{10,9... | collective-permute-start | bytes 786440 | tf_op jit(solution)/shard_map/ppermute | solution.py:14
  19.9 16.6 %collective-permute-start.1 = (bf16[16,32,256]{2,1,0:T(8,128)(2,1)S(1)}, bf16[16,32,256]{2,1,0:T(8,128)(2,1)S(1)}, u32[]{:S(2)}, u32[]{:S(2)}) collective-permute-start(bf16[16,32,256]{2,1,0:T(8,128)(2,1)S(1)} %collective-permute-done), channel_id=1, source_target_pairs={{0,7},{1,0},{2,1},{3,2},{4,3},{5,4},{6,5},{7,6},{8,15},{9,8},{10,9... | collective-permute-start | bytes 786440 | tf_op jit(solution)/shard_map/ppermute | solution.py:14
  36.5 16.5 %collective-permute-start.2 = (bf16[16,32,256]{2,1,0:T(8,128)(2,1)S(1)}, bf16[16,32,256]{2,1,0:T(8,128)(2,1)S(1)}, u32[]{:S(2)}, u32[]{:S(2)}) collective-permute-start(bf16[16,32,256]{2,1,0:T(8,128)(2,1)S(1)} %collective-permute-done.1), channel_id=1, source_target_pairs={{0,7},{1,0},{2,1},{3,2},{4,3},{5,4},{6,5},{7,6},{8,15},{9,8},{10,9... | collective-permute-start | bytes 786440 | tf_op jit(solution)/shard_map/ppermute | solution.py:14
  53.0 16.2 %collective-permute-start.3 = (bf16[16,32,256]{2,1,0:T(8,128)(2,1)S(1)}, bf16[16,32,256]{2,1,0:T(8,128)(2,1)S(1)}, u32[]{:S(2)}, u32[]{:S(2)}) collective-permute-start(bf16[16,32,256]{2,1,0:T(8,128)(2,1)S(1)} %collective-permute-done.2), channel_id=1, source_target_pairs={{0,7},{1,0},{2,1},{3,2},{4,3},{5,4},{6,5},{7,6},{8,15},{9,8},{10,9... | collective-permute-start | bytes 786440 | tf_op jit(solution)/shard_map/ppermute | solution.py:14
  69.2 15.9 %collective-permute-start.4 = (bf16[16,32,256]{2,1,0:T(8,128)(2,1)S(1)}, bf16[16,32,256]{2,1,0:T(8,128)(2,1)S(1)}, u32[]{:S(2)}, u32[]{:S(2)}) collective-permute-start(bf16[16,32,256]{2,1,0:T(8,128)(2,1)S(1)} %collective-permute-done.3), channel_id=1, source_target_pairs={{0,7},{1,0},{2,1},{3,2},{4,3},{5,4},{6,5},{7,6},{8,15},{9,8},{10,9... | collective-permute-start | bytes 786440 | tf_op jit(solution)/shard_map/ppermute | solution.py:14
  85.1 9.1 %collective-permute-start.5 = (bf16[16,32,256]{2,1,0:T(8,128)(2,1)S(1)}, bf16[16,32,256]{2,1,0:T(8,128)(2,1)S(1)}, u32[]{:S(2)}, u32[]{:S(2)}) collective-permute-start(bf16[16,32,256]{2,1,0:T(8,128)(2,1)S(1)} %collective-permute-done.4), channel_id=1, source_target_pairs={{0,7},{1,0},{2,1},{3,2},{4,3},{5,4},{6,5},{7,6},{8,15},{9,8},{10,9... | collective-permute-start | bytes 786440 | tf_op jit(solution)/shard_map/ppermute | solution.py:14
  94.2 14.9 %collective-permute-start.6 = (bf16[16,32,256]{2,1,0:T(8,128)(2,1)S(1)}, bf16[16,32,256]{2,1,0:T(8,128)(2,1)S(1)}, u32[]{:S(2)}, u32[]{:S(2)}) collective-permute-start(bf16[16,32,256]{2,1,0:T(8,128)(2,1)S(1)} %collective-permute-done.5), channel_id=1, source_target_pairs={{0,7},{1,0},{2,1},{3,2},{4,3},{5,4},{6,5},{7,6},{8,15},{9,8},{10,9... | collective-permute-start | bytes 786440 | tf_op jit(solution)/shard_map/ppermute | solution.py:14
  110.0 86.7 %copy-start.1 = (bf16[16,128,256]{2,1,0:T(8,128)(2,1)}, bf16[16,128,256]{2,1,0:T(8,128)(2,1)S(1)}, u32[]{:S(2)}) copy-start(bf16[16,128,256]{2,1,0:T(8,128)(2,1)S(1)} %add_convert_fusion) | copy-start | bytes 3145732
  188.1 6.3 %copy-start.2 = (bf16[16,5,256,256]{3,2,1,0:T(8,128)(2,1)S(1)}, bf16[16,5,256,256]{3,2,1,0:T(8,128)(2,1)}, u32[]{:S(2)}) copy-start(bf16[16,5,256,256]{3,2,1,0:T(8,128)(2,1)} %all-gather.2.cloned.1.call-done) | copy-start | bytes 31457284
  197.2 1.6 copy-start.5
  197.2 38.5 %copy-start.4 = (bf16[3,256,256]{2,1,0:T(8,128)(2,1)S(1)}, bf16[3,256,256]{2,1,0:T(8,128)(2,1)}, u32[]{:S(2)}) copy-start(bf16[3,256,256]{2,1,0:T(8,128)(2,1)} %param.12) | copy-start | bytes 1179652
  197.2 38.6 %copy-start.3 = (bf16[3,256,256]{2,1,0:T(8,128)(2,1)S(1)}, bf16[3,256,256]{2,1,0:T(8,128)(2,1)}, u32[]{:S(2)}) copy-start(bf16[3,256,256]{2,1,0:T(8,128)(2,1)} %param.13) | copy-start | bytes 1179652
Sparse Core Ops, SparseCore 0:
  10.2 177.8 all-gather.1
  198.9 34.7 all-reduce.1
